TPU v7x, 128 devices: a whole 4x4x4 slice. The times are simulated.
128 devices in a mesh: expert: 8 (over z, core), shard: 16 (over y, x).
Axes of the slice: x: 4, y: 4, z: 4, core: 2. Of those that a mesh axis runs over, the one named last changes fastest.
Arguments:
- tokens: bfloat16 [1024, 6144], P('expert'), may hold values from -6 to 6
- routes: int32 [1024, 2], P('expert'), may hold values from 0 to 7, all different within a row; in each aligned block of 128 rows (0 to 127, 128 to 255, ...) at most 64 rows name the same one
- route_weights: float32 [1024, 2], P('expert'), may hold values from 0.1 to 1
- out_grad: bfloat16 [1024, 6144], P('expert'), may hold values from -6 to 6
- w_gate: bfloat16 [8, 6144, 8192], P('expert', None, 'shard'), may hold values from -0.078125 to 0.078125
- w_up: bfloat16 [8, 6144, 8192], P('expert', None, 'shard'), may hold values from -0.078125 to 0.078125
- w_down: bfloat16 [8, 8192, 6144], P('expert', 'shard'), may hold values from -0.0625 to 0.0625
Outputs:
- moe_out: bfloat16 [1024, 6144], P('expert')
- input_grad: bfloat16 [1024, 6144], P('expert')
Inputs may be any that keep to these rules, and one draw needn't show every extreme that they name: `routes`: the two experts of a token differ. In each aligned block of 128 rows (the tokens of one expert group) no expert is named by more than 64 rows, and in every draw some expert is named by exactly 64 rows of some block.
All inputs are finite; a program needn't handle non-finite values.
Results may differ from a plain program's by a relative error of at most 0.02.
Values may be sent and summed in bfloat16 or wider, within the bound.
No kernel may reach another device: no remote copies, remote signals or barrier semaphores. Data moves between devices by JAX's collectives and lax.ppermute only.
A program may use at most 128 MiB of HBM per device.

v0:
```python
import jax
import jax.numpy as jnp
from jax import lax
from jax.sharding import PartitionSpec as P


def backward_terms(rows_g, gate_act, up_act, w_gate, w_up, w_down):
    contract = (((1,), (1,)), ((), ()))
    d_hidden = lax.dot_general(rows_g, w_down[0], contract, preferred_element_type=jnp.float32)
    sigmoid_g = jax.nn.sigmoid(gate_act)
    d_gate = (d_hidden * up_act * sigmoid_g * (1.0 + gate_act * (1.0 - sigmoid_g))).astype(
        jnp.bfloat16
    )
    d_up = (d_hidden * gate_act * sigmoid_g).astype(jnp.bfloat16)
    grad_part = lax.dot_general(d_gate, w_gate[0], contract, preferred_element_type=jnp.float32)
    return grad_part + lax.dot_general(d_up, w_up[0], contract, preferred_element_type=jnp.float32)


def weighted_pair(returned, target, route_weights, count_rows, model_width):
    flat_rows = returned.reshape(-1, model_width)
    chosen = flat_rows[target].reshape(count_rows, 2, model_width).astype(jnp.float32)
    total = route_weights[:, 0:1] * chosen[:, 0, :] + route_weights[:, 1:2] * chosen[:, 1, :]
    return total.astype(jnp.bfloat16)


def per_device(tokens, routes, route_weights, out_grad, w_gate, w_up, w_down):
    count_rows, model_width = tokens.shape
    groups = lax.axis_size("expert")
    per_expert = 4 * count_rows // groups
    slot_count = groups * per_expert
    picked = (routes[:, :, None] == jnp.arange(groups, dtype=jnp.int32)[None, None, :]).astype(
        jnp.int32
    )
    picked = picked.reshape(2 * count_rows, groups)
    before = jnp.sum((jnp.cumsum(picked, axis=0) - picked) * picked, axis=1)
    target = routes.reshape(-1) * per_expert + before
    matches = target[None, :] == jnp.arange(slot_count, dtype=jnp.int32)[:, None]
    placed = matches.reshape(slot_count, count_rows, 2)
    dispatch = jnp.any(placed, axis=2).astype(jnp.bfloat16)
    send_rows = (
        jnp.dot(dispatch, tokens, preferred_element_type=jnp.float32)
        .astype(jnp.bfloat16)
        .reshape(groups, per_expert, model_width)
    )
    send_grad = (
        jnp.dot(dispatch, out_grad, preferred_element_type=jnp.float32)
        .astype(jnp.bfloat16)
        .reshape(groups, per_expert, model_width)
    )
    rows_x, rows_g = (
        lax.all_to_all(send_rows, "expert", split_axis=0, concat_axis=0, tiled=True),
        lax.all_to_all(send_grad, "expert", split_axis=0, concat_axis=0, tiled=True),
    )
    rows_x = rows_x.reshape(slot_count, model_width)
    rows_g = rows_g.reshape(slot_count, model_width)
    gate_act = jnp.dot(rows_x, w_gate[0], preferred_element_type=jnp.float32)
    up_act = jnp.dot(rows_x, w_up[0], preferred_element_type=jnp.float32)
    hidden = (jax.nn.silu(gate_act) * up_act).astype(jnp.bfloat16)
    out_part = jnp.dot(hidden, w_down[0], preferred_element_type=jnp.float32).reshape(
        groups, per_expert, model_width
    )
    out_sum = lax.psum_scatter(
        out_part.astype(jnp.bfloat16), "shard", scatter_dimension=1, tiled=True
    )
    out_home = lax.all_to_all(out_sum, "expert", split_axis=0, concat_axis=0, tiled=True)
    out_back = lax.all_gather(out_home, "shard", axis=1, tiled=True)
    grad_part = backward_terms(rows_g, gate_act, up_act, w_gate, w_up, w_down).reshape(
        groups, per_expert, model_width
    )
    grad_sum = lax.psum_scatter(
        grad_part.astype(jnp.bfloat16), "shard", scatter_dimension=1, tiled=True
    )
    grad_home = lax.all_to_all(grad_sum, "expert", split_axis=0, concat_axis=0, tiled=True)
    grad_back = lax.all_gather(grad_home, "shard", axis=1, tiled=True)
    moe_out = weighted_pair(out_back, target, route_weights, count_rows, model_width)
    input_grad = weighted_pair(grad_back, target, route_weights, count_rows, model_width)
    return (moe_out, input_grad)


def solution(mesh):
    in_specs = (
        P("expert", None),
        P("expert", None),
        P("expert", None),
        P("expert", None),
        P("expert", None, "shard"),
        P("expert", None, "shard"),
        P("expert", "shard", None),
    )
    out_specs = (P("expert", None), P("expert", None))
    return jax.shard_map(
        per_device, mesh=mesh, in_specs=in_specs, out_specs=out_specs, check_vma=False
    )
```

profile of v0, /device:TPU:1, one launch (start us, length us, event | category | flops | bytes accessed | tf_op | source)
XLA Modules:
  0.0 559.2 jit_solution(7522904941379312739)
XLA Ops:
  9.6 4.4 convolution_convert_fusion.2
  14.0 6.9 %all-to-all-start = ((bf16[8,64,6144]{2,1,0:T(8,128)(2,1)}), bf16[8,64,6144]{2,1,0:T(8,128)(2,1)}, u32[]{:S(2)}, u32[]{:S(2)}) async-start(bf16[8,64,6144]{2,1,0:T(8,128)(2,1)} %bitcast.79), calls=%async_computation | async-start | bytes 12582912 | tf_op jit(solution)/shard_map/all_to_all | solution.py:51
  21.0 4.4 convolution_convert_fusion
  25.4 67.0 %all-to-all-done = bf16[8,64,6144]{2,1,0:T(8,128)(2,1)} async-done(((bf16[8,64,6144]{2,1,0:T(8,128)(2,1)}), bf16[8,64,6144]{2,1,0:T(8,128)(2,1)}, u32[]{:S(2)}, u32[]{:S(2)}) %all-to-all-start) | async-done | bytes 6291488 | tf_op jit(solution)/shard_map/all_to_all | solution.py:51
  92.3 5.5 all-to-all-start.2
  97.9 7.5 %fusion.8 = f32[512,512]{1,0:T(8,128)S(1)} fusion(bf16[512,6144]{1,0:T(8,128)(2,1)} %bitcast.4, bf16[1,6144,512]{2,1,0:T(8,128)(2,1)} %param.11), kind=kOutput, calls=%fused_computation.14 | convolution fusion | flops 3221225472 | bytes 13631488 | tf_op jit(solution)/shard_map/dot_general | solution.py:56
  105.4 8.2 %multiply_convert_fusion.2 = (bf16[512,512]{1,0:T(8,128)(2,1)S(1)}, f32[512,512]{1,0:T(8,128)S(1)}) fusion(f32[512,512]{1,0:T(8,128)S(1)} %fusion.8, bf16[512,6144]{1,0:T(8,128)(2,1)} %bitcast.4, bf16[1,6144,512]{2,1,0:T(8,128)(2,1)} %param.12), kind=kOutput, calls=%fused_computation.30 | convolution fusion | flops 3222798336 | bytes 15204352 | tf_op jit(solution)/shard_map/dot_general | solution.py:57
  113.5 55.8 %all-to-all-done.2 = bf16[8,64,6144]{2,1,0:T(8,128)(2,1)} async-done(((bf16[8,64,6144]{2,1,0:T(8,128)(2,1)}), bf16[8,64,6144]{2,1,0:T(8,128)(2,1)}, u32[]{:S(2)}, u32[]{:S(2)}) %all-to-all-start.2) | async-done | bytes 6291488 | tf_op jit(solution)/shard_map/all_to_all | solution.py:52
  169.3 7.5 %fusion.1 = f32[512,512]{1,0:T(8,128)S(1)} fusion(bf16[512,6144]{1,0:T(8,128)(2,1)} %bitcast.17, bf16[1,512,6144]{2,1,0:T(8,128)(2,1)} %param.13), kind=kOutput, calls=%fused_computation.7 | convolution fusion | flops 3221225472 | bytes 13631488 | tf_op jit(solution)/shard_map/dot_general | solution.py:9
  177.8 9.4 %fusion.6 = f32[512,6144]{1,0:T(8,128)} fusion(bf16[1,6144,512]{2,1,0:T(8,128)(2,1)} %param.11, f32[512,512]{1,0:T(8,128)S(1)} %fusion.8, f32[512,512]{1,0:T(8,128)S(1)} %fusion.1, f32[512,512]{1,0:T(8,128)S(1)} %get-tuple-element.13), kind=kOutput, calls=%fused_computation.12 | convolution fusion | flops 3223846912 | bytes 22020096 | tf_op jit(solution)/shard_map/dot_general | solution.py:15
  187.2 12.8 %add_convert_fusion = bf16[512,6144]{1,0:T(8,128)(2,1)} fusion(f32[512,6144]{1,0:T(8,128)} %fusion.6, bf16[1,6144,512]{2,1,0:T(8,128)(2,1)} %param.12, f32[512,512]{1,0:T(8,128)} %copy-done.3, f32[512,512]{1,0:T(8,128)S(1)} %fusion.8), kind=kOutput, calls=%fused_computation.2 | convolution fusion | flops 3229089792 | bytes 27262976 | tf_op jit(solution)/shard_map/dot_general | solution.py:16
  199.9 8.9 %copy.57 = bf16[8,64,6144]{2,0,1:T(8,128)(2,1)} copy(bf16[8,64,6144]{2,1,0:T(8,128)(2,1)} %bitcast.80) | data formatting | bytes 12582912 | tf_op jit(solution)/shard_map/convert_element_type | solution.py:71
  208.9 6.4 %convolution_convert_fusion.1 = bf16[8,64,6144]{2,1,0:T(8,128)(2,1)S(1)} fusion(bf16[8,64,512]{2,1,0:T(8,128)(2,1)S(1)} %bitcast.83, bf16[1,512,6144]{2,1,0:T(8,128)(2,1)} %param.13), kind=kOutput, calls=%fused_computation.4 | convolution fusion | flops 3224371200 | bytes 13107200 | tf_op jit(solution)/shard_map/dot_general | solution.py:59
  215.3 6.0 %copy.51 = bf16[8,64,6144]{2,0,1:T(8,128)(2,1)} copy(bf16[8,64,6144]{2,1,0:T(8,128)(2,1)S(1)} %convolution_convert_fusion.1) | data formatting | bytes 12582912 | tf_op jit(solution)/shard_map/convert_element_type | solution.py:63
  221.6 67.2 %reduce-scatter.5.cloned.1.call-done = bf16[8,4,6144]{2,0,1:T(8,128)(2,1)} async-done(((bf16[8,64,6144]{2,0,1:T(8,128)(2,1)}), bf16[8,4,6144]{2,0,1:T(8,128)(2,1)}) %reduce-scatter.5.cloned.1.call-update) | async-done | bytes 393232 | tf_op jit(solution)/shard_map/reduce_scatter | solution.py:70
  288.9 1.3 copy.58
  290.2 14.1 %all_to_all.20 = bf16[8,4,6144]{2,1,0:T(4,128)(2,1)S(1)} all-to-all(bf16[8,4,6144]{2,1,0:T(4,128)(2,1)S(1)} %copy.58), channel_id=1, replica_groups=mesh['expert'=8,'shard'=16] {'expert'}, dimensions={0} | all-to-all | bytes 786432 | tf_op jit(solution)/shard_map/all_to_all | solution.py:73
  304.3 1.0 copy.59
  305.3 67.7 %reduce-scatter.3.cloned.1.call-done = bf16[8,4,6144]{2,0,1:T(8,128)(2,1)} async-done(((bf16[8,64,6144]{2,0,1:T(8,128)(2,1)}), bf16[8,4,6144]{2,0,1:T(8,128)(2,1)}) %reduce-scatter.3.cloned.1.call-update) | async-done | bytes 393232 | tf_op jit(solution)/shard_map/reduce_scatter | solution.py:62
  373.0 1.3 copy.52
  374.3 14.1 %all_to_all.21 = bf16[8,4,6144]{2,1,0:T(4,128)(2,1)S(1)} all-to-all(bf16[8,4,6144]{2,1,0:T(4,128)(2,1)S(1)} %copy.52), channel_id=1, replica_groups=mesh['expert'=8,'shard'=16] {'expert'}, dimensions={0} | all-to-all | bytes 786432 | tf_op jit(solution)/shard_map/all_to_all | solution.py:65
  388.3 1.0 copy.53
  389.5 47.9 %all-gather.5.cloned.1.call-done = bf16[8,64,6144]{2,0,1:T(8,128)(2,1)} async-done(((bf16[8,4,6144]{2,0,1:T(8,128)(2,1)}), bf16[8,64,6144]{2,0,1:T(8,128)(2,1)}) %all-gather.5.cloned.1.call-update) | async-done | bytes 6291472 | tf_op jit(solution)/shard_map/all_gather | solution.py:74
  437.4 8.8 %copy.60 = bf16[8,64,6144]{2,1,0:T(8,128)(2,1)} copy(bf16[8,64,6144]{2,0,1:T(8,128)(2,1)} %all-gather.5.cloned.1.call-done) | data formatting | bytes 12582912 | tf_op jit(solution)/shard_map/all_gather | solution.py:74
  446.2 10.7 %gather_fusion.1 = bf16[256,6144]{1,0:T(8,128)(2,1)} fusion(bf16[512,6144]{1,0:T(8,128)(2,1)} %bitcast.77, s32[1024]{0:T(1024)S(1)} %pad_clamp_fusion), kind=kCustom, calls=%fused_computation.1 | custom fusion | bytes 6292480 | tf_op jit(solution)/shard_map/gather | solution.py:21
  456.9 8.0 %reshape.104 = f32[128,2,6144]{2,1,0:T(2,128)} reshape(bf16[256,6144]{1,0:T(8,128)(2,1)} %gather_fusion.1) | data formatting | bytes 9437184 | tf_op jit(solution)/shard_map/convert_element_type | solution.py:21
  465.0 36.0 %all-gather.3.cloned.1.call-done = bf16[8,64,6144]{2,0,1:T(8,128)(2,1)} async-done(((bf16[8,4,6144]{2,0,1:T(8,128)(2,1)}), bf16[8,64,6144]{2,0,1:T(8,128)(2,1)}) %all-gather.3.cloned.1.call-update) | async-done | bytes 6291472 | tf_op jit(solution)/shard_map/all_gather | solution.py:66
  500.9 8.8 %copy.54 = bf16[8,64,6144]{2,1,0:T(8,128)(2,1)} copy(bf16[8,64,6144]{2,0,1:T(8,128)(2,1)} %all-gather.3.cloned.1.call-done) | data formatting | bytes 12582912 | tf_op jit(solution)/shard_map/all_gather | solution.py:66
  509.7 10.7 %gather_fusion = bf16[256,6144]{1,0:T(8,128)(2,1)} fusion(bf16[512,6144]{1,0:T(8,128)(2,1)} %bitcast.76, s32[1024]{0:T(1024)S(1)} %pad_clamp_fusion), kind=kCustom, calls=%fused_computation | custom fusion | bytes 6292480 | tf_op jit(solution)/shard_map/gather | solution.py:21
  520.5 7.6 %reshape.103 = f32[128,2,6144]{2,1,0:T(2,128)} reshape(bf16[256,6144]{1,0:T(8,128)(2,1)} %gather_fusion) | data formatting | bytes 9437184 | tf_op jit(solution)/shard_map/convert_element_type | solution.py:21
  528.1 16.2 %fusion.27 = (f32[128,1,6144]{2,1,0:T(1,128)S(1)}, f32[128,1,6144]{2,1,0:T(1,128)S(1)}, f32[128,1,6144]{2,1,0:T(1,128)S(1)}, f32[128,1,6144]{2,1,0:T(1,128)S(1)}) fusion(f32[128,2,6144]{2,1,0:T(2,128)} %reshape.104, f32[128,2,6144]{2,1,0:T(2,128)} %reshape.103), kind=kLoop, calls=%fused_computation.51 | loop fusion | bytes 25165824 | tf_op jit(solution)/shard_map/slice | solution.py:22
  544.3 8.1 %fusion.12 = (bf16[128,6144]{1,0:T(8,128)(2,1)}, bf16[128,6144]{1,0:T(8,128)(2,1)}) fusion(f32[128,1,6144]{2,1,0:T(1,128)S(1)} %get-tuple-element.3, f32[128,1,6144]{2,1,0:T(1,128)S(1)} %get-tuple-element.2, f32[128]{0:T(128)S(1)} %get-tuple-element.11, f32[128]{0:T(128)S(1)} %get-tuple-element.10, f32[128,1,6144]{2,1,0:T(1,128)S(1)} %get-tuple-element.14, ...), kind=kLoop, calls=%fused_computation.19 | loop fusion | flops 6291456 | bytes 15729664 | tf_op jit(solution)/shard_map/convert_element_type | solution.py:23
  (35 shorter events, 4.0 us)
Async XLA Ops:
  7.2 2.5 copy-start
  14.0 7.0 %copy-start.2 = (bf16[128,6144]{1,0:T(8,128)(2,1)S(1)}, bf16[128,6144]{1,0:T(8,128)(2,1)}, u32[]{:S(2)}) copy-start(bf16[128,6144]{1,0:T(8,128)(2,1)} %param.10) | copy-start | bytes 4718596
  14.0 78.3 %all-to-all-start = ((bf16[8,64,6144]{2,1,0:T(8,128)(2,1)}), bf16[8,64,6144]{2,1,0:T(8,128)(2,1)}, u32[]{:S(2)}, u32[]{:S(2)}) async-start(bf16[8,64,6144]{2,1,0:T(8,128)(2,1)} %bitcast.79), calls=%async_computation | async-start | bytes 12582912 | tf_op jit(solution)/shard_map/all_to_all | solution.py:51
  92.3 76.9 %all-to-all-start.2 = ((bf16[8,64,6144]{2,1,0:T(8,128)(2,1)}), bf16[8,64,6144]{2,1,0:T(8,128)(2,1)}, u32[]{:S(2)}, u32[]{:S(2)}) async-start(bf16[8,64,6144]{2,1,0:T(8,128)(2,1)} %bitcast.78), calls=%async_computation.3 | async-start | bytes 12582912 | tf_op jit(solution)/shard_map/all_to_all | solution.py:52
  97.9 191.0 %reduce-scatter.5.cloned.1.call-start = ((), (), s32[]{:S(2)}) async-start(), calls=%async_computation.8 | async-start | bytes 6684672 | tf_op jit(solution)/shard_map/reduce_scatter | solution.py:70
  176.8 1.0 copy-start.3
  208.8 164.1 %reduce-scatter.3.cloned.1.call-start = ((), (), s32[]{:S(2)}) async-start(), calls=%async_computation.6 | async-start | bytes 6684672 | tf_op jit(solution)/shard_map/reduce_scatter | solution.py:62
  221.4 168.1 %copy-start.4 = (f32[128,2]{0,1:T(2,128)S(1)}, f32[128,2]{0,1:T(2,128)}, u32[]{:S(2)}) copy-start(f32[128,2]{0,1:T(2,128)} %param.9) | copy-start | bytes 3076
  221.4 216.0 %all-gather.5.cloned.1.call-start = ((), (), s32[]{:S(2)}) async-start(), calls=%async_computation.9 | async-start | bytes 6684672 | tf_op jit(solution)/shard_map/all_gather | solution.py:74
  305.2 195.7 %all-gather.3.cloned.1.call-start = ((), (), s32[]{:S(2)}) async-start(), calls=%async_computation.7 | async-start | bytes 6684672 | tf_op jit(solution)/shard_map/all_gather | solution.py:66
  544.3 8.1 %copy-start.1 = (bf16[128,6144]{1,0:T(8,128)(2,1)S(1)}, bf16[128,6144]{1,0:T(8,128)(2,1)}, u32[]{:S(2)}) copy-start(bf16[128,6144]{1,0:T(8,128)(2,1)} %param.7) | copy-start | bytes 4718596
Sparse Core Ops, SparseCore 0:
  208.9 79.8 reduce-scatter.4
  292.3 80.6 reduce-scatter.2
  375.7 61.6 all-gather.4
  440.0 60.9 all-gather.2
where the time goes:
time: 568 us; the launch traced here: 559 us
  waiting for transfers between devices  341 us (60%)
  local copies, waits for them, and re-layouts  93.1 us (16%)
  matrix products  60.5 us (11%)
  blocking collectives  28.2 us (5%)
  between operations  14.1 us (2%)
  starting transfers between devices  12.8 us (2%)
  other arithmetic  8.93 us (2%)
    reduce_scatter x1, waiting for transfers between devices, per_device(): lax.psum_scatter(out_part.astype(jnp.bfloat16), 'shard', scatter_dimensio...  67.7 us
    reduce_scatter x1, waiting for transfers between devices, per_device(): lax.psum_scatter(grad_part.astype(jnp.bfloat16), 'shard', scatter_dimensi...  67.2 us
    all_to_all x1, waiting for transfers between devices, per_device(): lax.all_to_all(send_rows, 'expert', split_axis=0, concat_axis=0, tiled=True)  67 us
    all_to_all x1, waiting for transfers between devices, per_device(): lax.all_to_all(send_grad, 'expert', split_axis=0, concat_axis=0, tiled=True)  55.8 us
    all_gather x1, waiting for transfers between devices, per_device(): grad_back = lax.all_gather(grad_home, 'shard', axis=1, tiled=True)  47.9 us
    all_gather x1, waiting for transfers between devices, per_device(): out_back = lax.all_gather(out_home, 'shard', axis=1, tiled=True)  36 us
    gather x2, local copies, waits for them, and re-layouts, weighted_pair(): flat_rows[target].reshape(count_rows, 2, model_width).astype(jnp.float32)  21.4 us
    slice x1, local copies, waits for them, and re-layouts, weighted_pair(): chosen[:, 0, :]  16.2 us
  transfers between devices with their start and end apart: 6, of which 6 were waited for; matrix products, arithmetic and copies ran while one was open for 12% of the time, Pallas kernels for 0%

commit v1 on v0

--- a/solution.py
+++ b/solution.py
@@ -71,7 +71,9 @@
         grad_part.astype(jnp.bfloat16), "shard", scatter_dimension=1, tiled=True
     )
     grad_home = lax.all_to_all(grad_sum, "expert", split_axis=0, concat_axis=0, tiled=True)
-    grad_back = lax.all_gather(grad_home, "shard", axis=1, tiled=True)
+    grad_back = jnp.concatenate(
+        lax.all_to_all(jnp.stack([grad_home] * lax.axis_size("shard")), "shard", 0, 0), axis=1
+    )
     moe_out = weighted_pair(out_back, target, route_weights, count_rows, model_width)
     input_grad = weighted_pair(grad_back, target, route_weights, count_rows, model_width)
     return (moe_out, input_grad)

time: 568 us -> 539 us (0.949)
  waiting for transfers between devices: 341 us -> 172 us
  blocking collectives: 28.2 us -> 181 us
  matrix products: 60.5 us -> 40.9 us
  local copies, waits for them, and re-layouts: 93.1 us -> 110 us
  starting transfers between devices: 12.8 us -> 4.92 us
    all_to_all x0 -> x2, blocking collectives: none -> 156 us  [the longest x1 79.1 us: per_device(): lax.all_to_all(send_rows, 'expert', split_axis=0, concat_axis=0, tiled=True)]
    reduce_scatter x1, waiting for transfers between devices: 67.7 us -> 0.02 us  [per_device(): lax.psum_scatter(out_part.astype(jnp.bfloat16), 'shard', scatter_dimensio...]
    all_gather x1 -> x0, waiting for transfers between devices: 47.9 us -> none  [per_device(): grad_back = lax.all_gather(grad_home, 'shard', axis=1, tiled=True)]
    all_gather x1, waiting for transfers between devices: 36 us -> 0.02 us  [per_device(): out_back = lax.all_gather(out_home, 'shard', axis=1, tiled=True)]
    all_to_all x2 -> x1, waiting for transfers between devices: 123 us -> 106 us  [per_device(): lax.all_to_all(jnp.stack([grad_home] * lax.axis_size('shard')), 'shard',...]
    another operation x1 -> x3, local copies, waits for them, and re-layouts: 0.01 us -> 16.2 us  [the longest x1 10.4 us: weighted_pair(): flat_rows = returned.reshape(-1, model_width)]
    reshape x0 -> x1, local copies, waits for them, and re-layouts: none -> 9.41 us  [per_device(): jnp.concatenate(lax.all_to_all(jnp.stack([grad_home] * lax.axis_size('sha...]
    all_gather x1 -> x0, local copies, waits for them, and re-layouts: 8.82 us -> none  [per_device(): grad_back = lax.all_gather(grad_home, 'shard', axis=1, tiled=True)]
  transfers between devices with their start and end apart: 6 -> 4, of which waited for: 6 -> 2; matrix products, arithmetic and copies ran while one was open for 12% -> 15% of each run, Pallas kernels for 0% -> 0%
where the time goes in v1:
time: 539 us; the launch traced here: 533 us
  blocking collectives  181 us (34%)
  waiting for transfers between devices  172 us (32%)
  local copies, waits for them, and re-layouts  110 us (20%)
  matrix products  40.9 us (8%)
  between operations  14.4 us (3%)
  other arithmetic  8.94 us (2%)
    all_to_all x1, waiting for transfers between devices, per_device(): lax.all_to_all(jnp.stack([grad_home] * lax.axis_size('shard')), 'shard',...  106 us
    all_to_all x1, blocking collectives, per_device(): lax.all_to_all(send_rows, 'expert', split_axis=0, concat_axis=0, tiled=True)  79.1 us
    all_to_all x1, blocking collectives, per_device(): lax.all_to_all(send_grad, 'expert', split_axis=0, concat_axis=0, tiled=True)  76.5 us
    reduce_scatter x1, waiting for transfers between devices, per_device(): lax.psum_scatter(grad_part.astype(jnp.bfloat16), 'shard', scatter_dimensi...  66 us
    gather x2, local copies, waits for them, and re-layouts, weighted_pair(): flat_rows[target].reshape(count_rows, 2, model_width).astype(jnp.float32)  21.5 us
    slice x1, local copies, waits for them, and re-layouts, weighted_pair(): chosen[:, 0, :]  16.2 us
    convert_element_type x2, local copies, waits for them, and re-layouts, weighted_pair(): flat_rows[target].reshape(count_rows, 2, model_width).astype(jnp.float32)  15.5 us
    all_to_all x1, blocking collectives, per_device(): lax.all_to_all(grad_sum, 'expert', split_axis=0, concat_axis=0, tiled=True)  14.1 us
  transfers between devices with their start and end apart: 4, of which 2 were waited for; matrix products, arithmetic and copies ran while one was open for 15% of the time, Pallas kernels for 0%

profile of v1, /device:TPU:1, one launch (start us, length us, event | category | flops | bytes accessed | tf_op | source)
XLA Modules:
  0.0 533.0 jit_solution(17366004538209256132)
XLA Ops:
  9.7 1.8 convolution_convert_fusion.2
  11.5 79.1 %all_to_all.25 = bf16[8,64,6144]{2,1,0:T(8,128)(2,1)S(1)} all-to-all(bf16[8,64,6144]{2,1,0:T(8,128)(2,1)S(1)} %bitcast.78), channel_id=1, replica_groups=mesh['expert'=8,'shard'=16] {'expert'}, dimensions={0} | all-to-all | bytes 12582912 | tf_op jit(solution)/shard_map/all_to_all | solution.py:51
  90.6 3.4 fusion.8
  94.0 7.4 %multiply_convert_fusion.2 = (bf16[512,512]{1,0:T(8,128)(2,1)S(1)}, f32[512,512]{1,0:T(8,128)}) fusion(f32[512,512]{1,0:T(8,128)S(1)} %fusion.8, bf16[512,6144]{1,0:T(8,128)(2,1)S(1)} %bitcast.80, bf16[1,6144,512]{2,1,0:T(8,128)(2,1)} %param.12), kind=kOutput, calls=%fused_computation.30 | convolution fusion | flops 3222798336 | bytes 15204352 | tf_op jit(solution)/shard_map/dot_general | solution.py:57
  101.4 3.6 convolution_convert_fusion.1
  105.0 6.0 %copy.51 = bf16[8,64,6144]{2,0,1:T(8,128)(2,1)} copy(bf16[8,64,6144]{2,1,0:T(8,128)(2,1)S(1)} %convolution_convert_fusion.1) | data formatting | bytes 12582912 | tf_op jit(solution)/shard_map/convert_element_type | solution.py:63
  111.1 1.3 copy-done.2
  112.5 1.8 convolution_convert_fusion
  114.3 76.5 %all_to_all.26 = bf16[8,64,6144]{2,1,0:T(8,128)(2,1)S(1)} all-to-all(bf16[8,64,6144]{2,1,0:T(8,128)(2,1)S(1)} %bitcast.77), channel_id=1, replica_groups=mesh['expert'=8,'shard'=16] {'expert'}, dimensions={0} | all-to-all | bytes 12582912 | tf_op jit(solution)/shard_map/all_to_all | solution.py:52
  190.8 3.4 fusion.1
  194.3 1.0 copy-done.4
  195.3 6.7 %fusion.6 = f32[512,6144]{1,0:T(8,128)} fusion(bf16[1,6144,512]{2,1,0:T(8,128)(2,1)S(1)} %bitcast.86, f32[512,512]{1,0:T(8,128)S(1)} %fusion.8, f32[512,512]{1,0:T(8,128)S(1)} %fusion.1, f32[512,512]{1,0:T(8,128)S(1)} %copy-done.3), kind=kOutput, calls=%fused_computation.12 | convolution fusion | flops 3223846912 | bytes 22020096 | tf_op jit(solution)/shard_map/dot_general | solution.py:15
  202.0 12.8 %add_convert_fusion = bf16[512,6144]{1,0:T(8,128)(2,1)} fusion(f32[512,6144]{1,0:T(8,128)} %fusion.6, bf16[1,6144,512]{2,1,0:T(8,128)(2,1)} %param.12, f32[512,512]{1,0:T(8,128)} %copy-done.4, f32[512,512]{1,0:T(8,128)S(1)} %fusion.8), kind=kOutput, calls=%fused_computation.2 | convolution fusion | flops 3229089792 | bytes 27262976 | tf_op jit(solution)/shard_map/dot_general | solution.py:16
  214.8 8.9 %copy.57 = bf16[8,64,6144]{2,0,1:T(8,128)(2,1)} copy(bf16[8,64,6144]{2,1,0:T(8,128)(2,1)} %bitcast.81) | data formatting | bytes 12582912 | tf_op jit(solution)/shard_map/convert_element_type | solution.py:71
  223.7 1.3 copy.52
  225.0 11.7 %all_to_all.27 = bf16[8,4,6144]{2,1,0:T(4,128)(2,1)S(1)} all-to-all(bf16[8,4,6144]{2,1,0:T(4,128)(2,1)S(1)} %copy.52), channel_id=1, replica_groups=mesh['expert'=8,'shard'=16] {'expert'}, dimensions={0} | all-to-all | bytes 786432 | tf_op jit(solution)/shard_map/all_to_all | solution.py:65
  236.7 1.0 copy.53
  237.7 66.0 %reduce-scatter.5.cloned.1.call-done = bf16[8,4,6144]{2,0,1:T(8,128)(2,1)} async-done(((bf16[8,64,6144]{2,0,1:T(8,128)(2,1)}), bf16[8,4,6144]{2,0,1:T(8,128)(2,1)}) %reduce-scatter.5.cloned.1.call-update) | async-done | bytes 393232 | tf_op jit(solution)/shard_map/reduce_scatter | solution.py:70
  303.7 1.3 copy.58
  305.0 14.1 %all_to_all.28 = bf16[8,4,6144]{2,1,0:T(4,128)(2,1)S(1)} all-to-all(bf16[8,4,6144]{2,1,0:T(4,128)(2,1)S(1)} %copy.58), channel_id=1, replica_groups=mesh['expert'=8,'shard'=16] {'expert'}, dimensions={0} | all-to-all | bytes 786432 | tf_op jit(solution)/shard_map/all_to_all | solution.py:73
  319.1 5.7 %stack.2 = bf16[16,8,4,6144]{3,2,1,0:T(4,128)(2,1)} broadcast(bf16[8,4,6144]{2,1,0:T(4,128)(2,1)S(1)} %all_to_all.28), dimensions={1,2,3} | broadcast | bytes 6684672 | tf_op jit(solution)/shard_map/stack | solution.py:75
  324.8 4.8 all-to-all-start.4
  329.8 106.2 %all-to-all-done.4 = bf16[16,8,4,6144]{3,2,1,0:T(4,128)(2,1)} async-done(((bf16[16,8,4,6144]{3,2,1,0:T(4,128)(2,1)}), bf16[16,8,4,6144]{3,2,1,0:T(4,128)(2,1)}, u32[]{:S(2)}, u32[]{:S(2)}) %all-to-all-start.4) | async-done | bytes 6291488 | tf_op jit(solution)/shard_map/all_to_all | solution.py:75
  436.0 9.4 %copy.59 = bf16[8,16,4,6144]{3,2,1,0:T(4,128)(2,1)} copy(bf16[8,16,4,6144]{3,2,0,1:T(4,128)(2,1)} %bitcast.19) | data formatting | bytes 12582912 | tf_op jit(solution)/shard_map/reshape | solution.py:74
  445.4 10.4 %reshape_reshape.3 = bf16[512,6144]{1,0:T(8,128)(2,1)} reshape(bf16[8,16,4,6144]{3,2,1,0:T(4,128)(2,1)} %copy.59) | data formatting | bytes 12582912 | tf_op jit(solution)/shard_map/reshape;reshape | solution.py:20
  455.8 10.7 %gather_fusion.1 = bf16[256,6144]{1,0:T(8,128)(2,1)} fusion(bf16[512,6144]{1,0:T(8,128)(2,1)} %reshape_reshape.3, s32[1024]{0:T(1024)S(1)} %pad_clamp_fusion), kind=kCustom, calls=%fused_computation.1 | custom fusion | bytes 6292480 | tf_op jit(solution)/shard_map/gather | solution.py:21
  466.6 7.8 %reshape.106 = f32[128,2,6144]{2,1,0:T(2,128)} reshape(bf16[256,6144]{1,0:T(8,128)(2,1)} %gather_fusion.1) | data formatting | bytes 9437184 | tf_op jit(solution)/shard_map/convert_element_type | solution.py:21
  474.4 8.8 %copy.54 = bf16[8,64,6144]{2,1,0:T(8,128)(2,1)} copy(bf16[8,64,6144]{2,0,1:T(8,128)(2,1)} %all-gather.2.cloned.1.call-done) | data formatting | bytes 12582912 | tf_op jit(solution)/shard_map/all_gather | solution.py:66
  483.3 10.7 %gather_fusion = bf16[256,6144]{1,0:T(8,128)(2,1)} fusion(bf16[512,6144]{1,0:T(8,128)(2,1)} %bitcast.76, s32[1024]{0:T(1024)S(1)} %pad_clamp_fusion), kind=kCustom, calls=%fused_computation | custom fusion | bytes 6292480 | tf_op jit(solution)/shard_map/gather | solution.py:21
  494.0 7.7 %reshape.105 = f32[128,2,6144]{2,1,0:T(2,128)} reshape(bf16[256,6144]{1,0:T(8,128)(2,1)} %gather_fusion) | data formatting | bytes 9437184 | tf_op jit(solution)/shard_map/convert_element_type | solution.py:21
  501.7 16.2 %fusion.27 = (f32[128,1,6144]{2,1,0:T(1,128)S(1)}, f32[128,1,6144]{2,1,0:T(1,128)S(1)}, f32[128,1,6144]{2,1,0:T(1,128)S(1)}, f32[128,1,6144]{2,1,0:T(1,128)S(1)}) fusion(f32[128,2,6144]{2,1,0:T(2,128)} %reshape.106, f32[128,2,6144]{2,1,0:T(2,128)} %reshape.105), kind=kLoop, calls=%fused_computation.51 | loop fusion | bytes 25165824 | tf_op jit(solution)/shard_map/slice | solution.py:22
  517.9 8.1 %fusion.12 = (bf16[128,6144]{1,0:T(8,128)(2,1)}, bf16[128,6144]{1,0:T(8,128)(2,1)}) fusion(f32[128,1,6144]{2,1,0:T(1,128)S(1)} %get-tuple-element.3, f32[128,1,6144]{2,1,0:T(1,128)S(1)} %get-tuple-element.2, f32[128]{0:T(128)S(1)} %get-tuple-element.11, f32[128]{0:T(128)S(1)} %get-tuple-element.10, f32[128,1,6144]{2,1,0:T(1,128)S(1)} %get-tuple-element.14, ...), kind=kLoop, calls=%fused_computation.19 | loop fusion | flops 6291456 | bytes 15729664 | tf_op jit(solution)/shard_map/convert_element_type | solution.py:23
  (55 shorter events, 2.9 us)
Async XLA Ops:
  7.2 2.5 copy-start
  7.2 216.5 %reduce-scatter.3.cloned.1.call-start = ((), (), s32[]{:S(2)}) async-start(), calls=%async_computation.7 | async-start | bytes 6684672 | tf_op jit(solution)/shard_map/reduce_scatter | solution.py:62
  9.7 80.9 %slice-start = ((s8[6291456]{0:T(1024)(128)(4,1)}), s8[4194304]{0:T(1024)(128)(4,1)S(1)}, s32[]{:S(2)}) async-start(s8[6291456]{0:T(1024)(128)(4,1)} %bitcast.83), calls=%async_computation.10 | async-start | bytes 8388608
  11.5 79.1 %slice-start.1 = ((s8[6291456]{0:T(1024)(128)(4,1)}), s8[2097152]{0:T(1024)(128)(4,1)S(1)}, s32[]{:S(2)}) async-start(s8[6291456]{0:T(1024)(128)(4,1)} %bitcast.83), calls=%async_computation.11 | async-start | bytes 4194304
  90.6 10.8 %slice-start.4 = ((s8[6291456]{0:T(1024)(128)(4,1)}), s8[4194304]{0:T(1024)(128)(4,1)S(1)}, s32[]{:S(2)}) async-start(s8[6291456]{0:T(1024)(128)(4,1)} %bitcast.89), calls=%async_computation.14 | async-start | bytes 8388608
  94.0 7.4 %slice-start.5 = ((s8[6291456]{0:T(1024)(128)(4,1)}), s8[2097152]{0:T(1024)(128)(4,1)S(1)}, s32[]{:S(2)}) async-start(s8[6291456]{0:T(1024)(128)(4,1)} %bitcast.89), calls=%async_computation.15 | async-start | bytes 4194304
  111.1 1.4 copy-start.2
  111.1 192.6 %reduce-scatter.5.cloned.1.call-start = ((), (), s32[]{:S(2)}) async-start(), calls=%async_computation.9 | async-start | bytes 6684672 | tf_op jit(solution)/shard_map/reduce_scatter | solution.py:70
  112.5 78.3 %slice-start.6 = ((s8[6291456]{0:T(1024)(128)(4,1)}), s8[4194304]{0:T(1024)(128)(4,1)S(1)}, s32[]{:S(2)}) async-start(s8[6291456]{0:T(1024)(128)(4,1)} %bitcast.91), calls=%async_computation.16 | async-start | bytes 8388608
  114.3 76.6 %slice-start.7 = ((s8[6291456]{0:T(1024)(128)(4,1)}), s8[2097152]{0:T(1024)(128)(4,1)S(1)}, s32[]{:S(2)}) async-start(s8[6291456]{0:T(1024)(128)(4,1)} %bitcast.91), calls=%async_computation.17 | async-start | bytes 4194304
  114.3 81.0 %slice-start.2 = ((s8[6291456]{0:T(1024)(128)(4,1)}), s8[4194304]{0:T(1024)(128)(4,1)S(1)}, s32[]{:S(2)}) async-start(s8[6291456]{0:T(1024)(128)(4,1)} %bitcast.85), calls=%async_computation.12 | async-start | bytes 8388608
  190.8 4.4 slice-start.3
  190.8 4.4 copy-start.3
  194.3 1.0 copy-start.4
  223.6 250.8 %all-gather.2.cloned.1.call-start = ((), (), s32[]{:S(2)}) async-start(), calls=%async_computation.8 | async-start | bytes 6684672 | tf_op jit(solution)/shard_map/all_gather | solution.py:66
  324.8 5.0 copy-start.5
  324.8 111.2 %all-to-all-start.4 = ((bf16[16,8,4,6144]{3,2,1,0:T(4,128)(2,1)}), bf16[16,8,4,6144]{3,2,1,0:T(4,128)(2,1)}, u32[]{:S(2)}, u32[]{:S(2)}) async-start(bf16[16,8,4,6144]{3,2,1,0:T(4,128)(2,1)} %stack.2), calls=%async_computation.6 | async-start | bytes 12582912 | tf_op jit(solution)/shard_map/all_to_all | solution.py:75
  517.9 8.1 %copy-start.1 = (bf16[128,6144]{1,0:T(8,128)(2,1)S(1)}, bf16[128,6144]{1,0:T(8,128)(2,1)}, u32[]{:S(2)}) copy-start(bf16[128,6144]{1,0:T(8,128)(2,1)} %param.7) | copy-start | bytes 4718596
Sparse Core Ops, SparseCore 0:
  111.2 79.9 reduce-scatter.2
  223.8 79.8 reduce-scatter.4
  306.4 130.3 all-gather.1
